TPU v7x, 32 devices: a whole 2x2x4 slice. The times are simulated.
32 devices in a mesh: parts: 2 (over x), blk: 8 (over z, y), clus: 2 (over core).
Axes of the slice: x: 2, y: 2, z: 4, core: 2. Of those that a mesh axis runs over, the one named last changes fastest.
Arguments:
- embeddings: bfloat16 [16384, 1024], P(('parts', 'blk', 'clus')), parts along dimension 0, as said below
- assignment: int32 [16384, 1], P(('parts', 'blk', 'clus')), parts along dimension 0, may hold values from 0 to 15; in each aligned block of 512 rows (0 to 511, 512 to 1023, ...) at most 128 rows name the same one
Outputs:
- prune_score: float32 [16384], P(('parts', 'blk', 'clus')), parts along dimension 0
There are 2 independent parts, one for each index of `parts`. A program takes and returns all parts, laid end to end along the dimension named above; each array names one. Nothing has to cross between parts.
Inputs may be any that keep to these rules, and one draw needn't show every extreme that they name: `assignment`: each document names one cluster; among the documents of one device no cluster is named by more than 128, and every cluster is named by some document. Real-valued embeddings; no row is zero.
All inputs are finite; a program needn't handle non-finite values.
Results may differ from a plain program's by a relative error of at most 0.0003.
Values may be sent and summed in bfloat16 or wider, within the bound.
A program may use at most 64 MiB of HBM per device.

v0:
```python
import jax
import jax.numpy as jnp
from jax import lax
from jax.sharding import PartitionSpec as P

kernel_scale = 4.0


def unit_rows(embeddings):
    widened = embeddings.astype(jnp.float32)
    normed = (
        widened
        * lax.rsqrt(jnp.mean(widened * widened, axis=1, keepdims=True) + 1e-06)
        * embeddings.shape[1] ** (-0.5)
    )
    return normed.astype(jnp.bfloat16)


def tile_density(queries, keys, key_weight):
    gram = lax.dot_general(
        queries, keys, (((1,), (1,)), ((), ())), preferred_element_type=jnp.float32
    )
    return jnp.sum(jnp.exp(kernel_scale * (gram - 1.0)) * key_weight[None, :], axis=1)


def per_device(embeddings, assignment):
    local_rows = embeddings.shape[0]
    feature_width = embeddings.shape[1]
    owners = lax.axis_size(("blk", "clus"))
    capacity = max(4 * local_rows // owners, 2)
    slot_total = owners * capacity
    tile_rows = min(512, slot_total)
    block_count = slot_total // tile_rows
    unit = unit_rows(embeddings)
    cluster = assignment[:, 0]
    onehot = (cluster[:, None] == jnp.arange(owners, dtype=jnp.int32)[None, :]).astype(jnp.int32)
    slot_rank = jnp.sum((jnp.cumsum(onehot, axis=0) - onehot) * onehot, axis=1)
    slot_index = cluster * capacity + slot_rank
    outgoing = jnp.zeros((slot_total, feature_width), jnp.bfloat16).at[slot_index].set(unit)
    occupied = jnp.zeros((slot_total,), jnp.int32).at[slot_index].set(1)
    incoming, arrived = (
        lax.all_to_all(
            outgoing.reshape(owners, capacity, feature_width),
            ("blk", "clus"),
            split_axis=0,
            concat_axis=0,
            tiled=True,
        ),
        lax.all_to_all(
            occupied.reshape(owners, capacity),
            ("blk", "clus"),
            split_axis=0,
            concat_axis=0,
            tiled=True,
        ),
    )
    incoming = incoming.reshape(slot_total, feature_width)
    arrived = arrived.reshape(slot_total)
    valid_weight = arrived.astype(jnp.float32)
    live_count = jnp.sum(valid_weight)

    def block_density(queries):
        return tile_density(queries, incoming, valid_weight)

    density = lax.map(
        block_density, incoming.reshape(block_count, tile_rows, feature_width)
    ).reshape(slot_total)
    slot_score = jnp.log(density / live_count)
    returned = lax.all_to_all(
        slot_score.reshape(owners, capacity),
        ("blk", "clus"),
        split_axis=0,
        concat_axis=0,
        tiled=True,
    )
    return returned.reshape(slot_total)[slot_index]


def solution(mesh):
    placed = (P(("parts", "blk", "clus"), None), P(("parts", "blk", "clus"), None))
    return jax.shard_map(
        per_device,
        mesh=mesh,
        in_specs=placed,
        out_specs=P(("parts", "blk", "clus")),
        check_vma=False,
    )
```

profile of v0, /device:TPU:0, one launch (start us, length us, event | category | flops | bytes accessed | tf_op | source)
XLA Modules:
  0.0 158.1 jit_solution(14365099038447796296)
XLA Ops:
  0.0 0.7 fusion.14
  0.7 1.1 reduce-window.6
  1.8 0.2 slice_reduce_fusion
  2.1 0.8 fusion.13
  2.9 0.7 compare_select_fusion
  3.6 3.0 %scatter_custom_fusion.1 = s32[2048]{0:T(1024)} fusion(s32[512]{0:T(512)S(1)} %bitcast.48, s32[512]{0:T(512)S(1)} %broadcast.62, s32[]{:T(128)} %constant.50.clone.1), kind=kCustom, calls=%fused_computation.28 | custom fusion | bytes 8196 | tf_op jit(solution)/shard_map/scatter | solution.py:40
  6.6 7.4 %all-to-all-start.1 = ((s32[16,1,128]{2,1,0:T(1,128)}), s32[16,1,128]{2,1,0:T(1,128)S(1)}, u32[]{:S(2)}, u32[]{:S(2)}) async-start(s32[16,1,128]{2,1,0:T(1,128)} %bitcast.10), calls=%async_computation.1 | async-start | bytes 16384 | tf_op jit(solution)/shard_map/all_to_all | solution.py:49
  14.0 1.5 fusion.3
  15.5 6.1 %scatter_custom_fusion = bf16[2048,1024]{1,0:T(8,128)(2,1)} fusion(s32[512]{0:T(512)S(1)} %bitcast.49, bf16[]{:T(256)} %constant.52.clone.1, bf16[512,1024]{1,0:T(8,128)(2,1)} %param.4, f32[]{:T(128)} %constant.57.clone.1, f32[512]{0:T(512)S(1)} %add_rsqrt_fusion), kind=kCustom, calls=%fused_computation.12 | custom fusion | flops 2097152 | bytes 5244934 | tf_op jit(solution)/shard_map/scatter | solution.py:39
  21.5 0.0 all-to-all-done.1
  21.5 6.1 %all-to-all-start = ((bf16[16,128,1024]{2,1,0:T(8,128)(2,1)}), bf16[16,128,1024]{2,1,0:T(8,128)(2,1)}, u32[]{:S(2)}, u32[]{:S(2)}) async-start(bf16[16,128,1024]{2,1,0:T(8,128)(2,1)} %bitcast.42), calls=%async_computation | async-start | bytes 8388608 | tf_op jit(solution)/shard_map/all_to_all | solution.py:42
  27.6 0.6 reduce_sum.44
  28.2 77.1 %all-to-all-done = bf16[16,128,1024]{2,1,0:T(8,128)(2,1)} async-done(((bf16[16,128,1024]{2,1,0:T(8,128)(2,1)}), bf16[16,128,1024]{2,1,0:T(8,128)(2,1)}, u32[]{:S(2)}, u32[]{:S(2)}) %all-to-all-start) | async-done | bytes 4194336 | tf_op jit(solution)/shard_map/all_to_all | solution.py:42
  105.3 21.3 %while.12 = (s32[]{:T(128)}, f32[4,512]{1,0:T(4,128)S(1)}, bf16[4,512,1024]{2,1,0:T(8,128)(2,1)}, bf16[2048,1024]{1,0:T(8,128)(2,1)}, f32[2048]{0:T(1024)S(1)}, /*index=5*/s32[]{:T(128)}, s32[]{:T(128)}) while((s32[]{:T(128)}, f32[4,512]{1,0:T(4,128)S(1)}, bf16[4,512,1024]{2,1,0:T(8,128)(2,1)}, bf16[2048,1024]{1,0:T(8,128)(2,1)}, ...), condition=%wide.region_8.9_spmd, body=%wide.region_6.8_spmd.sunk | while | flops 2151677440 | bytes 5257809 | solution.py:65
  105.3 5.3 %multiply_reduce_fusion.2 = f32[512]{0:T(512)S(1)} fusion(bf16[2048,1024]{1,0:T(8,128)(2,1)} %get-tuple-element.129, f32[2048]{0:T(1024)S(1)} %get-tuple-element.130, bf16[4,512,1024]{2,1,0:T(8,128)(2,1)} %get-tuple-element.128, s32[]{:T(128)} %get-tuple-element.119), kind=kOutput, calls=%fused_computation.3.clone.1 | convolution fusion | flops 2151677440 | bytes 5253632 | tf_op jit(solution)/shard_map/while/body/eval_jaxpr/dot_general | solution.py:20
  110.6 5.3 %multiply_reduce_fusion.2 = f32[512]{0:T(512)S(1)} fusion(bf16[2048,1024]{1,0:T(8,128)(2,1)} %get-tuple-element.129, f32[2048]{0:T(1024)S(1)} %get-tuple-element.130, bf16[4,512,1024]{2,1,0:T(8,128)(2,1)} %get-tuple-element.128, s32[]{:T(128)} %get-tuple-element.119), kind=kOutput, calls=%fused_computation.3.clone.1 | convolution fusion | flops 2151677440 | bytes 5253632 | tf_op jit(solution)/shard_map/while/body/eval_jaxpr/dot_general | solution.py:20
  115.9 5.3 %multiply_reduce_fusion.2 = f32[512]{0:T(512)S(1)} fusion(bf16[2048,1024]{1,0:T(8,128)(2,1)} %get-tuple-element.129, f32[2048]{0:T(1024)S(1)} %get-tuple-element.130, bf16[4,512,1024]{2,1,0:T(8,128)(2,1)} %get-tuple-element.128, s32[]{:T(128)} %get-tuple-element.119), kind=kOutput, calls=%fused_computation.3.clone.1 | convolution fusion | flops 2151677440 | bytes 5253632 | tf_op jit(solution)/shard_map/while/body/eval_jaxpr/dot_general | solution.py:20
  121.2 5.3 %multiply_reduce_fusion.2 = f32[512]{0:T(512)S(1)} fusion(bf16[2048,1024]{1,0:T(8,128)(2,1)} %get-tuple-element.129, f32[2048]{0:T(1024)S(1)} %get-tuple-element.130, bf16[4,512,1024]{2,1,0:T(8,128)(2,1)} %get-tuple-element.128, s32[]{:T(128)} %get-tuple-element.119), kind=kOutput, calls=%fused_computation.3.clone.1 | convolution fusion | flops 2151677440 | bytes 5253632 | tf_op jit(solution)/shard_map/while/body/eval_jaxpr/dot_general | solution.py:20
  126.5 0.6 divide_log_fusion
  127.1 0.6 log.15
  127.8 19.6 %all-to-all-start.2 = ((f32[16,1,128]{2,1,0:T(1,128)}), f32[16,1,128]{2,1,0:T(1,128)S(1)}, u32[]{:S(2)}, u32[]{:S(2)}) async-start(f32[16,1,128]{2,1,0:T(1,128)} %log.15), calls=%async_computation.2 | async-start | bytes 16384 | tf_op jit(solution)/shard_map/all_to_all | solution.py:69
  147.4 6.4 %all-to-all-done.2 = f32[16,1,128]{2,1,0:T(1,128)S(1)} async-done(((f32[16,1,128]{2,1,0:T(1,128)}), f32[16,1,128]{2,1,0:T(1,128)S(1)}, u32[]{:S(2)}, u32[]{:S(2)}) %all-to-all-start.2) | async-done | bytes 8224 | tf_op jit(solution)/shard_map/all_to_all | solution.py:69
  153.8 4.3 %gather_fusion = f32[512]{0:T(512)} fusion(f32[2048]{0:T(1024)S(1)} %bitcast.41, s32[1024]{0:T(1024)S(1)} %pad_clamp_fusion), kind=kCustom, calls=%fused_computation | custom fusion | bytes 6144 | tf_op jit(solution)/shard_map/gather | solution.py:76
  (11 shorter events, 0.3 us)
Async XLA Ops:
  6.6 15.0 %all-to-all-start.1 = ((s32[16,1,128]{2,1,0:T(1,128)}), s32[16,1,128]{2,1,0:T(1,128)S(1)}, u32[]{:S(2)}, u32[]{:S(2)}) async-start(s32[16,1,128]{2,1,0:T(1,128)} %bitcast.10), calls=%async_computation.1 | async-start | bytes 16384 | tf_op jit(solution)/shard_map/all_to_all | solution.py:49
  21.5 83.7 %all-to-all-start = ((bf16[16,128,1024]{2,1,0:T(8,128)(2,1)}), bf16[16,128,1024]{2,1,0:T(8,128)(2,1)}, u32[]{:S(2)}, u32[]{:S(2)}) async-start(bf16[16,128,1024]{2,1,0:T(8,128)(2,1)} %bitcast.42), calls=%async_computation | async-start | bytes 8388608 | tf_op jit(solution)/shard_map/all_to_all | solution.py:42
  127.8 26.1 %all-to-all-start.2 = ((f32[16,1,128]{2,1,0:T(1,128)}), f32[16,1,128]{2,1,0:T(1,128)S(1)}, u32[]{:S(2)}, u32[]{:S(2)}) async-start(f32[16,1,128]{2,1,0:T(1,128)} %log.15), calls=%async_computation.2 | async-start | bytes 16384 | tf_op jit(solution)/shard_map/all_to_all | solution.py:69
where the time goes:
time: 159 us; the launch traced here: 158 us
  waiting for transfers between devices  83.5 us (53%)
  starting transfers between devices  33.1 us (21%)
  matrix products  21 us (13%)
  other arithmetic  12.1 us (8%)
  local copies, waits for them, and re-layouts  8.31 us (5%)
    all_to_all x1, waiting for transfers between devices, per_device(): lax.all_to_all(outgoing.reshape(owners, capacity, feature_width), ('blk',...  77.1 us
    dot_general x4, matrix products, tile_density(): lax.dot_general(queries, keys, (((1,), (1,)), ((), ())), preferred_elemen...  21 us
    all_to_all x1, starting transfers between devices, per_device(): lax.all_to_all(slot_score.reshape(owners, capacity), ('blk', 'clus'), spl...  19.6 us
    all_to_all x1, starting transfers between devices, per_device(): lax.all_to_all(occupied.reshape(owners, capacity), ('blk', 'clus'), split...  7.39 us
    all_to_all x1, waiting for transfers between devices, per_device(): lax.all_to_all(slot_score.reshape(owners, capacity), ('blk', 'clus'), spl...  6.39 us
    all_to_all x1, starting transfers between devices, per_device(): lax.all_to_all(outgoing.reshape(owners, capacity, feature_width), ('blk',...  6.06 us
    scatter x1, other arithmetic, per_device(): jnp.zeros((slot_total, feature_width), jnp.bfloat16).at[slot_index]  6.05 us
    gather x1, local copies, waits for them, and re-layouts, per_device(): return returned.reshape(slot_total)[slot_index]  4.27 us
  transfers between devices with their start and end apart: 3, of which 2 were waited for; matrix products, arithmetic and copies ran while one was open for 5% of the time, Pallas kernels for 0%

commit v1 on v0

--- a/solution.py
+++ b/solution.py
@@ -1,9 +1,17 @@
+import functools
+
 import jax
 import jax.numpy as jnp
 from jax import lax
+from jax.experimental import pallas as pl
+from jax.experimental.pallas import tpu as pltpu
 from jax.sharding import PartitionSpec as P
 
 kernel_scale = 4.0
+MESH = pl.DeviceIdType.MESH
+CHUNKS = 4
+HALF = 256
+LANES = 128
 
 
 def unit_rows(embeddings):
@@ -16,6 +24,298 @@
     return normed.astype(jnp.bfloat16)
 
 
+def pair_kernel(
+    emb_ref, id_ref, out_ref,
+    line, plane, ids, id_cols, row_acc, line_part, plane_part, gathered,
+    line_send, line_recv, plane_send, plane_recv, id_send, id_recv, part_send, part_recv,
+):
+    tok, width = emb_ref.shape
+    rows = tok // CHUNKS
+    part, blk, core = lax.axis_index("parts"), lax.axis_index("blk"), lax.axis_index("clus")
+    z, y = blk // 2, blk % 2
+    flip = 1 - 2 * part
+    level = 3 * part + flip * z
+    me = blk * 2 + core
+    spot = y * 2 + core
+
+    def at_level(other, oy=None, ocore=None):
+        oz = 3 * part + flip * other
+        return (part, oz * 2 + (y if oy is None else oy), core if ocore is None else ocore)
+
+    def span(c):
+        return pl.ds(pl.multiple_of(c * rows, rows), rows)
+
+    def line_copy(source, c, target):
+        return pltpu.make_async_remote_copy(
+            src_ref=line.at[source, span(c)], dst_ref=line.at[source, span(c)],
+            send_sem=line_send.at[source, c], recv_sem=line_recv.at[source, c],
+            device_id=at_level(target), device_id_type=MESH)
+
+    def plane_copy(kind, slot, c, target):
+        return pltpu.make_async_remote_copy(
+            src_ref=plane.at[slot, span(c)], dst_ref=plane.at[slot, span(c)],
+            send_sem=plane_send.at[kind, c], recv_sem=plane_recv.at[slot, c],
+            device_id=target, device_id_type=MESH)
+
+    y_peer = at_level(level, oy=1 - y)
+    c_peer = at_level(level, ocore=1 - core)
+    y_spot = (1 - y) * 2 + core
+    c_spot = y * 2 + 1 - core
+    d_spot = (1 - y) * 2 + 1 - core
+    sends = ((level == 0) | (level == 1) | (level == 3))
+    target = jnp.where(level == 3, 2, level + 1)
+
+    barrier = pltpu.get_barrier_semaphore()
+
+    def other(k):
+        dev = (me + k) % 16
+        return dev, (part, dev // 2, dev % 2)
+
+    @pl.loop(1, 16)
+    def _(k):
+        pl.semaphore_signal(barrier, inc=1, device_id=other(k)[1], device_id_type=MESH)
+
+    ids[me] = id_ref[...]
+    row_acc[...] = jnp.zeros_like(row_acc)
+    pl.semaphore_wait(barrier, 15)
+
+    def id_copy(dev, at):
+        return pltpu.make_async_remote_copy(
+            src_ref=ids.at[me], dst_ref=ids.at[me],
+            send_sem=id_send.at[dev], recv_sem=id_recv.at[me],
+            device_id=at, device_id_type=MESH)
+
+    def id_arrival(dev):
+        return pltpu.make_async_remote_copy(
+            src_ref=ids.at[dev], dst_ref=ids.at[dev],
+            send_sem=id_send.at[dev], recv_sem=id_recv.at[dev],
+            device_id=other(1)[1], device_id_type=MESH)
+
+    @pl.loop(0, CHUNKS)
+    def _(c):
+        unit = unit_rows(emb_ref[span(c), :])
+        line[level, span(c)] = unit
+        plane[spot, span(c)] = unit
+
+        @pl.when(sends)
+        def _():
+            line_copy(level, c, target).start()
+        plane_copy(0, spot, c, y_peer).start()
+        plane_copy(1, spot, c, c_peer).start()
+
+    @pl.loop(1, 16)
+    def _(k):
+        dev, at = other(k)
+        id_copy(dev, at).start()
+
+    @pl.loop(1, 16)
+    def _(k):
+        id_arrival(other(k)[0]).wait_recv()
+
+    @pl.loop(0, 4)
+    def _(b):
+        row = jnp.broadcast_to(ids[(blk - y) * 2 + b], (LANES, tok))
+        id_cols[b] = row.T
+
+    own_ids = id_ref[...]
+
+    def count_cluster(d, total):
+        col = jnp.broadcast_to(ids[d], (LANES, tok)).T
+        parts = []
+        for s in range(tok // LANES):
+            same = col == own_ids[:, s * LANES:(s + 1) * LANES]
+            parts.append(jnp.sum(jnp.where(same, 1.0, 0.0), axis=0, keepdims=True))
+        return total + jnp.concatenate(parts, axis=1)
+
+    count = lax.fori_loop(0, 16, count_cluster, jnp.zeros((1, tok), jnp.float32))
+
+    @pl.loop(0, CHUNKS)
+    def _(c):
+        plane_copy(0, y_spot, c, y_peer).wait_recv()
+        plane_copy(2, y_spot, c, c_peer).start()
+
+        @pl.when((level == 1) | (level == 2))
+        def _():
+            line_copy(level - 1, c, target).wait_recv()
+            line_copy(level - 1, c, level + 1).start()
+
+    @pl.loop(0, CHUNKS)
+    def _(c):
+        plane_copy(1, c_spot, c, c_peer).wait_recv()
+        plane_copy(2, d_spot, c, c_peer).wait_recv()
+
+    steps = jnp.where(level == 0, 1, jnp.where(level == 1, 2, jnp.where(level == 2, 4, 3)))
+
+    def source_of(t):
+        at_two = jnp.where(t == 1, 1, jnp.where(t == 2, 3, 0))
+        at_three = jnp.where(t == 1, 1, 0)
+        later = jnp.where(level == 2, at_two, jnp.where(level == 3, at_three, 0))
+        return jnp.where(t == 0, level, later)
+
+    def part_copy(buffer, slot, sem, at):
+        return pltpu.make_async_remote_copy(
+            src_ref=buffer.at[slot], dst_ref=gathered.at[me],
+            send_sem=part_send.at[sem], recv_sem=part_recv.at[me],
+            device_id=at, device_id_type=MESH)
+
+    @pl.loop(0, steps)
+    def _(t):
+        source = source_of(t)
+        own = t == 0
+
+        @pl.when(level == 2)
+        def _():
+            line_copy(0, t, target).wait_recv()
+            line_copy(0, t, 3).start()
+
+        src_dev = (3 * part + flip * source) * 4 + spot
+        for h in range(tok // HALF):
+            @pl.when(((level == 3) & (t > 0)) | ((level == 2) & (t == 2)))
+            def _():
+                for c in range(h * HALF // rows, (h + 1) * HALF // rows):
+                    line_copy(source, c, target).wait_recv()
+
+            id_row = ids[src_dev][:, h * HALF:(h + 1) * HALF]
+
+            def meet(b, total):
+                block = line[source, h * HALF:(h + 1) * HALF, :]
+                gram = lax.dot_general(
+                    plane[b], block, (((1,), (1,)), ((), ())),
+                    preferred_element_type=jnp.float32)
+                value = jnp.exp(kernel_scale * (gram - 1.0))
+                col = id_cols[b]
+                sums, rowsum = [], None
+                for s in range(HALF // LANES):
+                    lanes = slice(s * LANES, (s + 1) * LANES)
+                    kept = jnp.where(col == id_row[:, lanes], value[:, lanes], 0.0)
+                    sums.append(jnp.sum(kept, axis=0, keepdims=True))
+                    rowsum = kept if rowsum is None else rowsum + kept
+
+                @pl.when(t > 0)
+                def _():
+                    row_acc[b] = row_acc[b] + rowsum
+                return total + jnp.concatenate(sums, axis=1)
+
+            line_part[source, :, h * HALF:(h + 1) * HALF] = lax.fori_loop(
+                0, 4, meet, jnp.zeros((1, HALF), jnp.float32))
+
+        @pl.when(t > 0)
+        def _():
+            part_copy(line_part, source, source, at_level(source)).start()
+
+    def plane_peer(k):
+        peer = (spot + k) % 4
+        return peer, at_level(level, oy=peer // 2, ocore=peer % 2)
+
+    @pl.when(level > 0)
+    def _():
+        for b in range(4):
+            plane_part[b] = jnp.sum(row_acc[b].T, axis=0, keepdims=True)
+        for k in range(1, 4):
+            peer, at = plane_peer(k)
+            part_copy(plane_part, peer, 4 + peer, at).start()
+
+    total = line_part[level]
+    out_ref[...] = total
+
+    def part_arrival(dev):
+        return pltpu.make_async_remote_copy(
+            src_ref=line_part.at[0], dst_ref=gathered.at[dev],
+            send_sem=part_send.at[0], recv_sem=part_recv.at[dev],
+            device_id=y_peer, device_id_type=MESH)
+
+    def take(source_level):
+        dev = (3 * part + flip * source_level) * 4 + spot
+        part_arrival(dev).wait_recv()
+        out_ref[...] = out_ref[...] + gathered[dev]
+
+    @pl.when(level == 0)
+    def _():
+        take(1)
+
+    @pl.when((level != 2))
+    def _():
+        take(2)
+
+    @pl.when(level < 2)
+    def _():
+        take(3)
+
+    @pl.when(level > 0)
+    def _():
+        out_ref[...] = out_ref[...] + plane_part[spot]
+        for k in range(1, 4):
+            dev = (blk - y) * 2 + plane_peer(k)[0]
+            part_arrival(dev).wait_recv()
+            out_ref[...] = out_ref[...] + gathered[dev]
+
+    out_ref[...] = jnp.log(out_ref[...] / count)
+
+    @pl.loop(1, 16)
+    def _(k):
+        dev, at = other(k)
+        id_copy(dev, at).wait_send()
+
+    @pl.loop(0, CHUNKS)
+    def _(c):
+        @pl.when(sends)
+        def _():
+            line_copy(level, c, target).wait_send()
+
+        @pl.when((level == 1) | (level == 2))
+        def _():
+            line_copy(level - 1, c, target).wait_send()
+
+        @pl.when(level == 2)
+        def _():
+            line_copy(0, c, target).wait_send()
+        plane_copy(0, spot, c, y_peer).wait_send()
+        plane_copy(1, spot, c, c_peer).wait_send()
+        plane_copy(2, y_spot, c, c_peer).wait_send()
+
+    @pl.loop(1, steps)
+    def _(t):
+        source = source_of(t)
+        part_copy(line_part, source, source, at_level(source)).wait_send()
+
+    @pl.when(level > 0)
+    def _():
+        for k in range(1, 4):
+            peer, at = plane_peer(k)
+            part_copy(plane_part, peer, 4 + peer, at).wait_send()
+
+
+def pair_scores(embeddings, assignment):
+    tok, width = embeddings.shape
+    score = pl.pallas_call(
+        pair_kernel,
+        out_shape=jax.ShapeDtypeStruct((1, tok), jnp.float32),
+        in_specs=[pl.BlockSpec(memory_space=pltpu.VMEM)] * 2,
+        out_specs=pl.BlockSpec(memory_space=pltpu.VMEM),
+        scratch_shapes=[
+            pltpu.VMEM((4, tok, width), jnp.bfloat16),
+            pltpu.VMEM((4, tok, width), jnp.bfloat16),
+            pltpu.VMEM((16, 1, tok), jnp.int32),
+            pltpu.VMEM((4, tok, LANES), jnp.int32),
+            pltpu.VMEM((4, tok, LANES), jnp.float32),
+            pltpu.VMEM((4, 1, tok), jnp.float32),
+            pltpu.VMEM((4, 1, tok), jnp.float32),
+            pltpu.VMEM((16, 1, tok), jnp.float32),
+            pltpu.SemaphoreType.DMA((4, CHUNKS)),
+            pltpu.SemaphoreType.DMA((4, CHUNKS)),
+            pltpu.SemaphoreType.DMA((3, CHUNKS)),
+            pltpu.SemaphoreType.DMA((4, CHUNKS)),
+            pltpu.SemaphoreType.DMA((16,)),
+            pltpu.SemaphoreType.DMA((16,)),
+            pltpu.SemaphoreType.DMA((8,)),
+            pltpu.SemaphoreType.DMA((16,)),
+        ],
+        compiler_params=pltpu.CompilerParams(
+            collective_id=0, has_side_effects=True, vmem_limit_bytes=40 << 20),
+    )(embeddings, assignment.reshape(1, tok))
+    return score.reshape(tok)
+
+
 def tile_density(queries, keys, key_weight):
     gram = lax.dot_general(
         queries, keys, (((1,), (1,)), ((), ())), preferred_element_type=jnp.float32
@@ -23,7 +323,7 @@
     return jnp.sum(jnp.exp(kernel_scale * (gram - 1.0)) * key_weight[None, :], axis=1)
 
 
-def per_device(embeddings, assignment):
+def routed_scores(embeddings, assignment):
     local_rows = embeddings.shape[0]
     feature_width = embeddings.shape[1]
     owners = lax.axis_size(("blk", "clus"))
@@ -78,8 +378,10 @@
 
 def solution(mesh):
     placed = (P(("parts", "blk", "clus"), None), P(("parts", "blk", "clus"), None))
+    sizes = (mesh.shape["parts"], mesh.shape["blk"], mesh.shape["clus"])
+    body = pair_scores if sizes == (2, 8, 2) else routed_scores
     return jax.shard_map(
-        per_device,
+        body,
         mesh=mesh,
         in_specs=placed,
         out_specs=P(("parts", "blk", "clus")),

time: 159 us -> 91.4 us (0.57)
  Pallas kernels: 0 us -> 88.7 us
  waiting for transfers between devices: 83.5 us -> 0 us
  starting transfers between devices: 33.1 us -> 0 us
  matrix products: 21 us -> 0 us
  other arithmetic: 12.1 us -> 0 us
  local copies, waits for them, and re-layouts: 8.31 us -> 2.49 us
    pallas_call x0 -> x1, Pallas kernels: none -> 88.7 us  [pair_scores(): pl.pallas_call(pair_kernel, out_shape=jax.ShapeDtypeStruct((1, tok), jnp....]
    all_to_all x3 -> x0, waiting for transfers between devices: 83.5 us -> none  [the longest x1 77.1 us: per_device(): lax.all_to_all(outgoing.reshape(owners, capacity, feature_width), ('blk',...]
    all_to_all x3 -> x0, starting transfers between devices: 33.1 us -> none  [the longest x1 19.6 us: per_device(): lax.all_to_all(slot_score.reshape(owners, capacity), ('blk', 'clus'), spl...]
    dot_general x4 -> x0, matrix products: 21 us -> none  [tile_density(): lax.dot_general(queries, keys, (((1,), (1,)), ((), ())), preferred_elemen...]
    scatter x1 -> x0, other arithmetic: 6.05 us -> none  [per_device(): jnp.zeros((slot_total, feature_width), jnp.bfloat16).at[slot_index]]
    gather x1 -> x0, local copies, waits for them, and re-layouts: 4.27 us -> none  [per_device(): return returned.reshape(slot_total)[slot_index]]
    scatter x1 -> x0, local copies, waits for them, and re-layouts: 3.01 us -> none  [per_device(): occupied = jnp.zeros((slot_total,), jnp.int32).at[slot_index].set(1)]
    reduce_sum x3 -> x0, other arithmetic: 2.86 us -> none  [the longest x1 1.5 us: unit_rows(): jnp.mean(widened * widened, axis=1, keepdims=True) + 1e-06]
  transfers between devices with their start and end apart: 3 -> 0, of which waited for: 2 -> 0; matrix products, arithmetic and copies ran while one was open for 5% -> 0% of each run, Pallas kernels for 0% -> 0%
where the time goes in v1:
time: 91.4 us; the launch traced here: 91.2 us
  Pallas kernels  88.7 us (97%)
  local copies, waits for them, and re-layouts  2.49 us (3%)
    pallas_call x1, Pallas kernels, pair_scores(): pl.pallas_call(pair_kernel, out_shape=jax.ShapeDtypeStruct((1, tok), jnp....  88.7 us
    unnamed x5, local copies, waits for them, and re-layouts  2.49 us

profile of v1, /device:TPU:0, one launch (start us, length us, event | category | flops | bytes accessed | tf_op | source)
XLA Modules:
  0.0 91.2 jit_solution(16885739675951677149)
XLA Ops:
  0.0 0.0 copy-start
  0.0 1.2 %copy-done = bf16[512,1024]{1,0:T(8,128)(2,1)S(1)} copy-done((bf16[512,1024]{1,0:T(8,128)(2,1)S(1)}, bf16[512,1024]{1,0:T(8,128)(2,1)}, u32[]{:S(2)}) %copy-start) | copy-done | bytes 1048600
  1.2 0.0 copy-start.1
  1.2 0.7 copy-done.1
  1.9 88.7 %shard_map.28 = f32[1,512]{1,0:T(1,128)S(1)} custom-call(bf16[512,1024]{1,0:T(8,128)(2,1)S(1)} %copy-done, s32[1,512]{1,0:T(1,128)S(1)} %bitcast.3), custom_call_target="tpu_custom_call" | custom-call | tf_op jit(solution)/shard_map/pallas_call | solution.py:290
  90.7 0.6 copy.4
Async XLA Ops:
  0.0 1.2 %copy-start = (bf16[512,1024]{1,0:T(8,128)(2,1)S(1)}, bf16[512,1024]{1,0:T(8,128)(2,1)}, u32[]{:S(2)}) copy-start(bf16[512,1024]{1,0:T(8,128)(2,1)} %emb_ref.1) | copy-start | bytes 3145732
  1.2 0.7 copy-start.1

commit v2 on v1

--- a/solution.py
+++ b/solution.py
@@ -9,9 +9,30 @@
 
 kernel_scale = 4.0
 MESH = pl.DeviceIdType.MESH
-CHUNKS = 4
+CHUNKS = 8
+ROUNDS = 11
+RELAYED = 6
 HALF = 256
 LANES = 128
+JOBS = (
+    ((1, 0, 0, 0), (2, 0, 1, 0), (9, 0, 0, 1), (10, 0, 1, 1)),
+    ((1, 1, 0, 0), (2, 1, 1, 0), (8, 0, 0, 0), (9, 1, 0, 1), (9, 1, 1, 1), (10, 0, 0, 1), (10, 0, 1, 0), (10, 0, 1, 1)),
+    ((1, 2, 0, 0), (2, 2, 1, 0), (5, 1, 0, 0), (7, 3, 0, 0), (8, 0, 0, 0), (9, 1, 1, 0), (9, 2, 0, 1), (9, 2, 1, 1),
+     (10, 1, 0, 1), (10, 1, 1, 1), (10, 3, 0, 1), (10, 0, 0, 1), (10, 3, 1, 0), (10, 3, 1, 1), (10, 0, 1, 0), (10, 0, 1, 1)),
+    ((1, 3, 0, 0), (2, 3, 1, 0), (7, 1, 0, 0), (8, 1, 1, 0), (9, 3, 0, 1), (9, 3, 1, 1), (9, 1, 0, 1), (10, 1, 1, 1),
+     (10, 0, 0, 0), (10, 0, 0, 1), (10, 0, 1, 0), (10, 0, 1, 1)),
+)
+
+
+def pick(table, index):
+    value = jnp.int32(table[-1])
+    for k in reversed(range(len(table) - 1)):
+        value = jnp.where(index == k, table[k], value)
+    return value
+
+
+def pick_level(tables, level, index):
+    return pick([pick(t, index) for t in tables], level)
 
 
 def unit_rows(embeddings):
@@ -26,8 +47,9 @@
 
 def pair_kernel(
     emb_ref, id_ref, out_ref,
-    line, plane, ids, id_cols, row_acc, line_part, plane_part, gathered,
+    line, plane, relay, ids, id_cols, row_acc, line_part, plane_part, gathered,
     line_send, line_recv, plane_send, plane_recv, id_send, id_recv, part_send, part_recv,
+    relay_send, relay_recv, x_send,
 ):
     tok, width = emb_ref.shape
     rows = tok // CHUNKS
@@ -62,8 +84,6 @@
     y_spot = (1 - y) * 2 + core
     c_spot = y * 2 + 1 - core
     d_spot = (1 - y) * 2 + 1 - core
-    sends = ((level == 0) | (level == 1) | (level == 3))
-    target = jnp.where(level == 3, 2, level + 1)
 
     barrier = pltpu.get_barrier_semaphore()
 
@@ -75,9 +95,12 @@
     def _(k):
         pl.semaphore_signal(barrier, inc=1, device_id=other(k)[1], device_id_type=MESH)
 
+    x_peer = (1 - part, blk, core)
+    pl.semaphore_signal(barrier, inc=1, device_id=x_peer, device_id_type=MESH)
     ids[me] = id_ref[...]
+    line_part[...] = jnp.zeros_like(line_part)
     row_acc[...] = jnp.zeros_like(row_acc)
-    pl.semaphore_wait(barrier, 15)
+    pl.semaphore_wait(barrier, 16)
 
     def id_copy(dev, at):
         return pltpu.make_async_remote_copy(
@@ -90,23 +113,147 @@
             src_ref=ids.at[dev], dst_ref=ids.at[dev],
             send_sem=id_send.at[dev], recv_sem=id_recv.at[dev],
             device_id=other(1)[1], device_id_type=MESH)
+
+    @pl.loop(1, 16)
+    def _(k):
+        dev, at = other(k)
+        id_copy(dev, at).start()
+
+    def up_copy(i):
+        first = (level == 0) | (i < 4)
+        source = jnp.where(first, jnp.minimum(level, 1), 0)
+        return line_copy(source, jnp.where(first, i, i - 4), level + 1)
+
+    def up_round(r):
+        i = r - level // 2
+
+        @pl.when((level < 3) & (i >= 0) & (i < jnp.where(level == 0, 8, 10)))
+        def _():
+            @pl.when((level == 2) | ((level == 1) & (i >= 4)))
+            def _():
+                up_copy(i).wait_recv()
+
+            @pl.when(i > 0)
+            def _():
+                up_copy(i - 1).wait_send()
+            up_copy(i).start()
+
+    def relay_copy(j):
+        return pltpu.make_async_remote_copy(
+            src_ref=relay.at[j], dst_ref=relay.at[j],
+            send_sem=relay_send.at[j], recv_sem=relay_recv.at[j],
+            device_id=at_level(level - 1), device_id_type=MESH)
+
+    def down_round(r):
+        @pl.when((level == 3) & (r < 10))
+        def _():
+            own = jnp.where(r < 2, r, r - 2)
+
+            @pl.when((r == 2) | (r == 3))
+            def _():
+                @pl.when(r == 2)
+                def _():
+                    line_copy(3, 1, 2).wait_send()
+
+                @pl.when(r == 3)
+                def _():
+                    relay_copy(4).wait_send()
+                relay_copy(r + 2).wait_recv()
+                relay_copy(r + 2).start()
+
+            @pl.when((r < 2) | (r > 3))
+            def _():
+                @pl.when(r == 4)
+                def _():
+                    relay_copy(5).wait_send()
+
+                @pl.when((r == 1) | (r > 4))
+                def _():
+                    line_copy(3, own - 1, 2).wait_send()
+                line_copy(3, own, 2).start()
+
+        i = r - (3 - level)
+
+        @pl.when(((level == 1) | (level == 2)) & (i >= 0) & (i < RELAYED))
+        def _():
+            relay_copy(i).wait_recv()
+
+            @pl.when(i > 0)
+            def _():
+                relay_copy(i - 1).wait_send()
+            relay_copy(i).start()
+
+    def out_copy(i):
+        j = jnp.where(level == 0, 4 + i, i)
+        return pltpu.make_async_remote_copy(
+            src_ref=line.at[level, span(jnp.where(level == 0, 6 + i, 4 + i))], dst_ref=relay.at[j],
+            send_sem=x_send.at[i], recv_sem=relay_recv.at[j],
+            device_id=x_peer, device_id_type=MESH)
+
+    def back_copy(i):
+        j = jnp.where(level == 0, i - 2, i - 4)
+        source = jnp.where(j < 4, 1, 0)
+        at = span(jnp.where(j < 4, j + 4, j + 2))
+        return pltpu.make_async_remote_copy(
+            src_ref=relay.at[j], dst_ref=line.at[source, at],
+            send_sem=x_send.at[i], recv_sem=line_recv.at[source, jnp.where(j < 4, j + 4, j + 2)],
+            device_id=x_peer, device_id_type=MESH)
+
+    def x_round(r):
+        i = jnp.where((level == 0) & (r > 1), r - 1, r)
+        outs = jnp.where(level == 0, 2, 4)
+        total = jnp.where(level == 0, 8, 10)
+
+        @pl.when((level < 2) & (i < total) & ((level == 1) | (r != 2)))
+        def _():
+            @pl.when(i > outs)
+            def _():
+                back_copy(i - 1).wait_send()
+
+            @pl.when((i > 0) & (i <= outs))
+            def _():
+                out_copy(i - 1).wait_send()
+
+            @pl.when(i < outs)
+            def _():
+                out_copy(i).start()
+
+            @pl.when(i >= outs)
+            def _():
+                @pl.when(level == 0)
+                def _():
+                    relay_copy(i - 2).wait_recv()
+                back_copy(i).start()
+
+    def y_round(r):
+        @pl.when(r < CHUNKS)
+        def _():
+            @pl.when(r > 0)
+            def _():
+                plane_copy(0, spot, r - 1, y_peer).wait_send()
+            plane_copy(0, spot, r, y_peer).start()
+
+    def y_pass(r):
+        @pl.when((r > 0) & (r <= CHUNKS))
+        def _():
+            plane_copy(0, y_spot, r - 1, y_peer).wait_recv()
+            plane_copy(2, y_spot, r - 1, c_peer).start()
 
     @pl.loop(0, CHUNKS)
     def _(c):
         unit = unit_rows(emb_ref[span(c), :])
         line[level, span(c)] = unit
         plane[spot, span(c)] = unit
-
-        @pl.when(sends)
-        def _():
-            line_copy(level, c, target).start()
-        plane_copy(0, spot, c, y_peer).start()
         plane_copy(1, spot, c, c_peer).start()
 
-    @pl.loop(1, 16)
-    def _(k):
-        dev, at = other(k)
-        id_copy(dev, at).start()
+    def comm(r):
+        y_round(r)
+        x_round(r)
+        up_round(r)
+        down_round(r)
+        y_pass(r)
+
+    comm(0)
 
     @pl.loop(1, 16)
     def _(k):
@@ -129,21 +276,6 @@
 
     count = lax.fori_loop(0, 16, count_cluster, jnp.zeros((1, tok), jnp.float32))
 
-    @pl.loop(0, CHUNKS)
-    def _(c):
-        plane_copy(0, y_spot, c, y_peer).wait_recv()
-        plane_copy(2, y_spot, c, c_peer).start()
-
-        @pl.when((level == 1) | (level == 2))
-        def _():
-            line_copy(level - 1, c, target).wait_recv()
-            line_copy(level - 1, c, level + 1).start()
-
-    @pl.loop(0, CHUNKS)
-    def _(c):
-        plane_copy(1, c_spot, c, c_peer).wait_recv()
-        plane_copy(2, d_spot, c, c_peer).wait_recv()
-
     steps = jnp.where(level == 0, 1, jnp.where(level == 1, 2, jnp.where(level == 2, 4, 3)))
 
     def source_of(t):
@@ -158,50 +290,74 @@
             send_sem=part_send.at[sem], recv_sem=part_recv.at[me],
             device_id=at, device_id_type=MESH)
 
-    @pl.loop(0, steps)
+    starts = [[sum(1 for job in jobs if job[0] < r) for r in range(ROUNDS + 1)] for jobs in JOBS]
+
+    def job(n):
+        source = pick_level([[j[1] for j in jobs] for jobs in JOBS], level, n)
+        h = pick_level([[j[2] for j in jobs] for jobs in JOBS], level, n)
+        pair = pick_level([[j[3] for j in jobs] for jobs in JOBS], level, n)
+        first = CHUNKS // 2 * h
+
+        @pl.when((pair == 0) & (source != level))
+        def _():
+            everything = (level == 3) | (source == 3)
+            low = jnp.where(everything, 0, jnp.where((source == 0) & (h == 1), 2, 0))
+            high = jnp.where(everything | (h == 1), CHUNKS // 2, 0)
+
+            @pl.loop(low, high)
+            def _(c):
+                line_copy(source, first + c, 0).wait_recv()
+
+        src_dev = (3 * part + flip * source) * 4 + spot
+        at = pl.ds(pl.multiple_of(h * HALF, HALF), HALF)
+        id_row = ids[src_dev, :, at]
+
+        def meet(k, total):
+            b = (y + pair) % 2 * 2 + k
+            gram = lax.dot_general(
+                plane[b], line[source, at, :], (((1,), (1,)), ((), ())),
+                preferred_element_type=jnp.float32)
+            value = jnp.exp(kernel_scale * (gram - 1.0))
+            col = id_cols[b]
+            sums, rowsum = [], None
+            for s in range(HALF // LANES):
+                lanes = slice(s * LANES, (s + 1) * LANES)
+                kept = jnp.where(col == id_row[:, lanes], value[:, lanes], 0.0)
+                sums.append(jnp.sum(kept, axis=0, keepdims=True))
+                rowsum = kept if rowsum is None else rowsum + kept
+
+            @pl.when(source != level)
+            def _():
+                row_acc[b] = row_acc[b] + rowsum
+            return total + jnp.concatenate(sums, axis=1)
+
+        line_part[source, :, at] = line_part[source, :, at] + lax.fori_loop(
+            0, 2, meet, jnp.zeros((1, HALF), jnp.float32))
+
+    @pl.loop(1, ROUNDS)
+    def _(r):
+        comm(r)
+
+        @pl.when(r == 1)
+        def _():
+            @pl.loop(0, CHUNKS)
+            def _(c):
+                plane_copy(1, c_spot, c, c_peer).wait_recv()
+
+        @pl.when(r == 9)
+        def _():
+            @pl.loop(0, CHUNKS)
+            def _(c):
+                plane_copy(2, d_spot, c, c_peer).wait_recv()
+
+        @pl.loop(pick_level(starts, level, r), pick_level(starts, level, r + 1))
+        def _(n):
+            job(n)
+
+    @pl.loop(1, steps)
     def _(t):
         source = source_of(t)
-        own = t == 0
-
-        @pl.when(level == 2)
-        def _():
-            line_copy(0, t, target).wait_recv()
-            line_copy(0, t, 3).start()
-
-        src_dev = (3 * part + flip * source) * 4 + spot
-        for h in range(tok // HALF):
-            @pl.when(((level == 3) & (t > 0)) | ((level == 2) & (t == 2)))
-            def _():
-                for c in range(h * HALF // rows, (h + 1) * HALF // rows):
-                    line_copy(source, c, target).wait_recv()
-
-            id_row = ids[src_dev][:, h * HALF:(h + 1) * HALF]
-
-            def meet(b, total):
-                block = line[source, h * HALF:(h + 1) * HALF, :]
-                gram = lax.dot_general(
-                    plane[b], block, (((1,), (1,)), ((), ())),
-                    preferred_element_type=jnp.float32)
-                value = jnp.exp(kernel_scale * (gram - 1.0))
-                col = id_cols[b]
-                sums, rowsum = [], None
-                for s in range(HALF // LANES):
-                    lanes = slice(s * LANES, (s + 1) * LANES)
-                    kept = jnp.where(col == id_row[:, lanes], value[:, lanes], 0.0)
-                    sums.append(jnp.sum(kept, axis=0, keepdims=True))
-                    rowsum = kept if rowsum is None else rowsum + kept
-
-                @pl.when(t > 0)
-                def _():
-                    row_acc[b] = row_acc[b] + rowsum
-                return total + jnp.concatenate(sums, axis=1)
-
-            line_part[source, :, h * HALF:(h + 1) * HALF] = lax.fori_loop(
-                0, 4, meet, jnp.zeros((1, HALF), jnp.float32))
-
-        @pl.when(t > 0)
-        def _():
-            part_copy(line_part, source, source, at_level(source)).start()
+        part_copy(line_part, source, source, at_level(source)).start()
 
     def plane_peer(k):
         peer = (spot + k) % 4
@@ -258,20 +414,25 @@
 
     @pl.loop(0, CHUNKS)
     def _(c):
-        @pl.when(sends)
-        def _():
-            line_copy(level, c, target).wait_send()
-
-        @pl.when((level == 1) | (level == 2))
-        def _():
-            line_copy(level - 1, c, target).wait_send()
-
-        @pl.when(level == 2)
-        def _():
-            line_copy(0, c, target).wait_send()
-        plane_copy(0, spot, c, y_peer).wait_send()
         plane_copy(1, spot, c, c_peer).wait_send()
         plane_copy(2, y_spot, c, c_peer).wait_send()
+    plane_copy(0, spot, CHUNKS - 1, y_peer).wait_send()
+
+    @pl.when(level < 3)
+    def _():
+        up_copy(jnp.where(level == 0, 7, 9)).wait_send()
+
+    @pl.when(level == 3)
+    def _():
+        line_copy(3, CHUNKS - 1, 2).wait_send()
+
+    @pl.when((level == 1) | (level == 2))
+    def _():
+        relay_copy(RELAYED - 1).wait_send()
+
+    @pl.when(level < 2)
+    def _():
+        back_copy(jnp.where(level == 0, 7, 9)).wait_send()
 
     @pl.loop(1, steps)
     def _(t):
@@ -295,6 +456,7 @@
         scratch_shapes=[
             pltpu.VMEM((4, tok, width), jnp.bfloat16),
             pltpu.VMEM((4, tok, width), jnp.bfloat16),
+            pltpu.VMEM((RELAYED, tok // CHUNKS, width), jnp.bfloat16),
             pltpu.VMEM((16, 1, tok), jnp.int32),
             pltpu.VMEM((4, tok, LANES), jnp.int32),
             pltpu.VMEM((4, tok, LANES), jnp.float32),
@@ -309,6 +471,9 @@
             pltpu.SemaphoreType.DMA((16,)),
             pltpu.SemaphoreType.DMA((8,)),
             pltpu.SemaphoreType.DMA((16,)),
+            pltpu.SemaphoreType.DMA((RELAYED,)),
+            pltpu.SemaphoreType.DMA((RELAYED,)),
+            pltpu.SemaphoreType.DMA((10,)),
         ],
         compiler_params=pltpu.CompilerParams(
             collective_id=0, has_side_effects=True, vmem_limit_bytes=40 << 20),

time: 91.4 us -> 60.2 us (0.66)
  Pallas kernels: 88.7 us -> 57.5 us
    pallas_call x1, Pallas kernels: 88.7 us -> 57.5 us  [pair_scores(): pl.pallas_call(pair_kernel, out_shape=jax.ShapeDtypeStruct((1, tok), jnp....]
where the time goes in v2:
time: 60.2 us; the launch traced here: 60 us
  Pallas kernels  57.5 us (96%)
  local copies, waits for them, and re-layouts  2.49 us (4%)
    pallas_call x1, Pallas kernels, pair_scores(): pl.pallas_call(pair_kernel, out_shape=jax.ShapeDtypeStruct((1, tok), jnp....  57.5 us
    unnamed x5, local copies, waits for them, and re-layouts  2.49 us

profile of v2, /device:TPU:0, one launch (start us, length us, event | category | flops | bytes accessed | tf_op | source)
XLA Modules:
  0.0 60.0 jit_solution(539903904689475517)
XLA Ops:
  0.0 0.0 copy-start
  0.0 1.2 %copy-done = bf16[512,1024]{1,0:T(8,128)(2,1)S(1)} copy-done((bf16[512,1024]{1,0:T(8,128)(2,1)S(1)}, bf16[512,1024]{1,0:T(8,128)(2,1)}, u32[]{:S(2)}) %copy-start) | copy-done | bytes 1048600
  1.2 0.0 copy-start.1
  1.2 0.7 %copy-done.1 = s32[512,1]{0,1:T(1,128)S(1)} copy-done((s32[512,1]{0,1:T(1,128)S(1)}, s32[512,1]{0,1:T(1,128)}, u32[]{:S(2)}) %copy-start.1) | copy-done | bytes 2072
  1.9 57.5 %shard_map.28 = f32[1,512]{1,0:T(1,128)S(1)} custom-call(bf16[512,1024]{1,0:T(8,128)(2,1)S(1)} %copy-done, s32[1,512]{1,0:T(1,128)S(1)} %bitcast.3), custom_call_target="tpu_custom_call" | custom-call | tf_op jit(solution)/shard_map/pallas_call | solution.py:451
  59.5 0.6 copy.4
Async XLA Ops:
  0.0 1.2 %copy-start = (bf16[512,1024]{1,0:T(8,128)(2,1)S(1)}, bf16[512,1024]{1,0:T(8,128)(2,1)}, u32[]{:S(2)}) copy-start(bf16[512,1024]{1,0:T(8,128)(2,1)} %emb_ref.1) | copy-start | bytes 3145732
  1.2 0.7 %copy-start.1 = (s32[512,1]{0,1:T(1,128)S(1)}, s32[512,1]{0,1:T(1,128)}, u32[]{:S(2)}) copy-start(s32[512,1]{0,1:T(1,128)} %param.3) | copy-start | bytes 6148

commit v3 on v2

--- a/solution.py
+++ b/solution.py
@@ -1,4 +1,5 @@
 import functools
+import math
 
 import jax
 import jax.numpy as jnp
@@ -11,6 +12,7 @@
 MESH = pl.DeviceIdType.MESH
 CHUNKS = 8
 ROUNDS = 11
+DEPTH = 2
 RELAYED = 6
 HALF = 256
 LANES = 128
@@ -46,12 +48,16 @@
 
 
 def pair_kernel(
-    emb_ref, id_ref, out_ref,
-    line, plane, relay, ids, id_cols, row_acc, line_part, plane_part, gathered,
+    emb_hbm, id_hbm, out_ref,
+    emb_ref, id_ref, line, plane, relay, count_ref, ids, id_cols, row_acc, line_part, plane_part, gathered,
     line_send, line_recv, plane_send, plane_recv, id_send, id_recv, part_send, part_recv,
-    relay_send, relay_recv, x_send,
+    relay_send, relay_recv, x_send, load_sem,
 ):
     tok, width = emb_ref.shape
+    load_ids = pltpu.make_async_copy(id_hbm, id_ref, load_sem.at[0])
+    load_rows = pltpu.make_async_copy(emb_hbm, emb_ref, load_sem.at[1])
+    load_ids.start()
+    load_rows.start()
     rows = tok // CHUNKS
     part, blk, core = lax.axis_index("parts"), lax.axis_index("blk"), lax.axis_index("clus")
     z, y = blk // 2, blk % 2
@@ -67,6 +73,9 @@
     def span(c):
         return pl.ds(pl.multiple_of(c * rows, rows), rows)
 
+    def plane_span(slot, c):
+        return pl.ds(pl.multiple_of(slot * tok + c * rows, rows), rows)
+
     def line_copy(source, c, target):
         return pltpu.make_async_remote_copy(
             src_ref=line.at[source, span(c)], dst_ref=line.at[source, span(c)],
@@ -75,7 +84,7 @@
 
     def plane_copy(kind, slot, c, target):
         return pltpu.make_async_remote_copy(
-            src_ref=plane.at[slot, span(c)], dst_ref=plane.at[slot, span(c)],
+            src_ref=plane.at[plane_span(slot, c)], dst_ref=plane.at[plane_span(slot, c)],
             send_sem=plane_send.at[kind, c], recv_sem=plane_recv.at[slot, c],
             device_id=target, device_id_type=MESH)
 
@@ -97,9 +106,18 @@
 
     x_peer = (1 - part, blk, core)
     pl.semaphore_signal(barrier, inc=1, device_id=x_peer, device_id_type=MESH)
+    load_ids.wait()
     ids[me] = id_ref[...]
     line_part[...] = jnp.zeros_like(line_part)
     row_acc[...] = jnp.zeros_like(row_acc)
+    load_rows.wait()
+
+    @pl.loop(0, CHUNKS)
+    def _(c):
+        unit = unit_rows(emb_ref[span(c), :])
+        line[level, span(c)] = unit
+        plane[plane_span(spot, c)] = unit
+
     pl.semaphore_wait(barrier, 16)
 
     def id_copy(dev, at):
@@ -133,9 +151,9 @@
             def _():
                 up_copy(i).wait_recv()
 
-            @pl.when(i > 0)
-            def _():
-                up_copy(i - 1).wait_send()
+            @pl.when(i >= DEPTH)
+            def _():
+                up_copy(i - DEPTH).wait_send()
             up_copy(i).start()
 
     def relay_copy(j):
@@ -144,33 +162,40 @@
             send_sem=relay_send.at[j], recv_sem=relay_recv.at[j],
             device_id=at_level(level - 1), device_id_type=MESH)
 
+    def own_down(i):
+        return line_copy(3, jnp.where(i < 2, i, i - 2), 2)
+
+    def down_sent(i):
+        passed = (i == 2) | (i == 3)
+
+        @pl.when(passed)
+        def _():
+            relay_copy(i + 2).wait_send()
+
+        @pl.when(jnp.logical_not(passed))
+        def _():
+            own_down(i).wait_send()
+
     def down_round(r):
         @pl.when((level == 3) & (r < 10))
         def _():
-            own = jnp.where(r < 2, r, r - 2)
-
-            @pl.when((r == 2) | (r == 3))
-            def _():
-                @pl.when(r == 2)
-                def _():
-                    line_copy(3, 1, 2).wait_send()
-
-                @pl.when(r == 3)
-                def _():
-                    relay_copy(4).wait_send()
+            passed = (r == 2) | (r == 3)
+
+            @pl.when(passed)
+            def _():
                 relay_copy(r + 2).wait_recv()
+
+            @pl.when(r >= DEPTH)
+            def _():
+                down_sent(r - DEPTH)
+
+            @pl.when(passed)
+            def _():
                 relay_copy(r + 2).start()
 
-            @pl.when((r < 2) | (r > 3))
-            def _():
-                @pl.when(r == 4)
-                def _():
-                    relay_copy(5).wait_send()
-
-                @pl.when((r == 1) | (r > 4))
-                def _():
-                    line_copy(3, own - 1, 2).wait_send()
-                line_copy(3, own, 2).start()
+            @pl.when(jnp.logical_not(passed))
+            def _():
+                own_down(r).start()
 
         i = r - (3 - level)
 
@@ -178,9 +203,9 @@
         def _():
             relay_copy(i).wait_recv()
 
-            @pl.when(i > 0)
-            def _():
-                relay_copy(i - 1).wait_send()
+            @pl.when(i >= DEPTH)
+            def _():
+                relay_copy(i - DEPTH).wait_send()
             relay_copy(i).start()
 
     def out_copy(i):
@@ -199,6 +224,12 @@
             send_sem=x_send.at[i], recv_sem=line_recv.at[source, jnp.where(j < 4, j + 4, j + 2)],
             device_id=x_peer, device_id_type=MESH)
 
+    def x_sent(i):
+        pltpu.make_async_remote_copy(
+            src_ref=relay.at[0], dst_ref=relay.at[0],
+            send_sem=x_send.at[i], recv_sem=relay_recv.at[0],
+            device_id=x_peer, device_id_type=MESH).wait_send()
+
     def x_round(r):
         i = jnp.where((level == 0) & (r > 1), r - 1, r)
         outs = jnp.where(level == 0, 2, 4)
@@ -206,13 +237,9 @@
 
         @pl.when((level < 2) & (i < total) & ((level == 1) | (r != 2)))
         def _():
-            @pl.when(i > outs)
-            def _():
-                back_copy(i - 1).wait_send()
-
-            @pl.when((i > 0) & (i <= outs))
-            def _():
-                out_copy(i - 1).wait_send()
+            @pl.when(i >= DEPTH)
+            def _():
+                x_sent(i - DEPTH)
 
             @pl.when(i < outs)
             def _():
@@ -228,9 +255,9 @@
     def y_round(r):
         @pl.when(r < CHUNKS)
         def _():
-            @pl.when(r > 0)
-            def _():
-                plane_copy(0, spot, r - 1, y_peer).wait_send()
+            @pl.when(r >= DEPTH)
+            def _():
+                plane_copy(0, spot, r - DEPTH, y_peer).wait_send()
             plane_copy(0, spot, r, y_peer).start()
 
     def y_pass(r):
@@ -241,9 +268,6 @@
 
     @pl.loop(0, CHUNKS)
     def _(c):
-        unit = unit_rows(emb_ref[span(c), :])
-        line[level, span(c)] = unit
-        plane[spot, span(c)] = unit
         plane_copy(1, spot, c, c_peer).start()
 
     def comm(r):
@@ -262,7 +286,7 @@
     @pl.loop(0, 4)
     def _(b):
         row = jnp.broadcast_to(ids[(blk - y) * 2 + b], (LANES, tok))
-        id_cols[b] = row.T
+        id_cols[pl.ds(pl.multiple_of(b * tok, tok), tok), :] = row.T
 
     own_ids = id_ref[...]
 
@@ -274,7 +298,7 @@
             parts.append(jnp.sum(jnp.where(same, 1.0, 0.0), axis=0, keepdims=True))
         return total + jnp.concatenate(parts, axis=1)
 
-    count = lax.fori_loop(0, 16, count_cluster, jnp.zeros((1, tok), jnp.float32))
+    count_ref[...] = jnp.zeros_like(count_ref)
 
     steps = jnp.where(level == 0, 1, jnp.where(level == 1, 2, jnp.where(level == 2, 4, 3)))
 
@@ -312,31 +336,32 @@
         at = pl.ds(pl.multiple_of(h * HALF, HALF), HALF)
         id_row = ids[src_dev, :, at]
 
-        def meet(k, total):
-            b = (y + pair) % 2 * 2 + k
-            gram = lax.dot_general(
-                plane[b], line[source, at, :], (((1,), (1,)), ((), ())),
-                preferred_element_type=jnp.float32)
-            value = jnp.exp(kernel_scale * (gram - 1.0))
-            col = id_cols[b]
-            sums, rowsum = [], None
-            for s in range(HALF // LANES):
-                lanes = slice(s * LANES, (s + 1) * LANES)
-                kept = jnp.where(col == id_row[:, lanes], value[:, lanes], 0.0)
-                sums.append(jnp.sum(kept, axis=0, keepdims=True))
-                rowsum = kept if rowsum is None else rowsum + kept
-
-            @pl.when(source != level)
-            def _():
-                row_acc[b] = row_acc[b] + rowsum
-            return total + jnp.concatenate(sums, axis=1)
-
-        line_part[source, :, at] = line_part[source, :, at] + lax.fori_loop(
-            0, 2, meet, jnp.zeros((1, HALF), jnp.float32))
+        two = pl.ds(pl.multiple_of((y + pair) % 2 * 2 * tok, 2 * tok), 2 * tok)
+        gram = lax.dot_general(
+            plane[two, :], line[source, at, :], (((1,), (1,)), ((), ())),
+            preferred_element_type=jnp.float32)
+        value = jnp.exp2((kernel_scale * math.log2(math.e)) * (gram - 1.0))
+        col = id_cols[two, :]
+        sums, rowsum = [], None
+        for s in range(HALF // LANES):
+            lanes = slice(s * LANES, (s + 1) * LANES)
+            kept = jnp.where(col == id_row[:, lanes], value[:, lanes], 0.0)
+            sums.append(jnp.sum(kept, axis=0, keepdims=True))
+            rowsum = kept if rowsum is None else rowsum + kept
+
+        @pl.when(source != level)
+        def _():
+            row_acc[two, :] = row_acc[two, :] + rowsum
+
+        line_part[source, :, at] = line_part[source, :, at] + jnp.concatenate(sums, axis=1)
 
     @pl.loop(1, ROUNDS)
     def _(r):
         comm(r)
+
+        @pl.when(r <= 8)
+        def _():
+            count_ref[...] = lax.fori_loop(2 * r - 2, 2 * r, count_cluster, count_ref[...])
 
         @pl.when(r == 1)
         def _():
@@ -366,7 +391,7 @@
     @pl.when(level > 0)
     def _():
         for b in range(4):
-            plane_part[b] = jnp.sum(row_acc[b].T, axis=0, keepdims=True)
+            plane_part[b] = jnp.sum(row_acc[b * tok:(b + 1) * tok, :].T, axis=0, keepdims=True)
         for k in range(1, 4):
             peer, at = plane_peer(k)
             part_copy(plane_part, peer, 4 + peer, at).start()
@@ -405,7 +430,7 @@
             part_arrival(dev).wait_recv()
             out_ref[...] = out_ref[...] + gathered[dev]
 
-    out_ref[...] = jnp.log(out_ref[...] / count)
+    out_ref[...] = jnp.log(out_ref[...] / count_ref[...])
 
     @pl.loop(1, 16)
     def _(k):
@@ -416,23 +441,26 @@
     def _(c):
         plane_copy(1, spot, c, c_peer).wait_send()
         plane_copy(2, y_spot, c, c_peer).wait_send()
-    plane_copy(0, spot, CHUNKS - 1, y_peer).wait_send()
-
-    @pl.when(level < 3)
-    def _():
-        up_copy(jnp.where(level == 0, 7, 9)).wait_send()
-
-    @pl.when(level == 3)
-    def _():
-        line_copy(3, CHUNKS - 1, 2).wait_send()
-
-    @pl.when((level == 1) | (level == 2))
-    def _():
-        relay_copy(RELAYED - 1).wait_send()
-
-    @pl.when(level < 2)
-    def _():
-        back_copy(jnp.where(level == 0, 7, 9)).wait_send()
+
+    @pl.loop(0, DEPTH)
+    def _(k):
+        plane_copy(0, spot, CHUNKS - 1 - k, y_peer).wait_send()
+
+        @pl.when(level < 3)
+        def _():
+            up_copy(jnp.where(level == 0, 7, 9) - k).wait_send()
+
+        @pl.when(level == 3)
+        def _():
+            down_sent(9 - k)
+
+        @pl.when((level == 1) | (level == 2))
+        def _():
+            relay_copy(RELAYED - 1 - k).wait_send()
+
+        @pl.when(level < 2)
+        def _():
+            x_sent(jnp.where(level == 0, 7, 9) - k)
 
     @pl.loop(1, steps)
     def _(t):
@@ -451,15 +479,18 @@
     score = pl.pallas_call(
         pair_kernel,
         out_shape=jax.ShapeDtypeStruct((1, tok), jnp.float32),
-        in_specs=[pl.BlockSpec(memory_space=pltpu.VMEM)] * 2,
+        in_specs=[pl.BlockSpec(memory_space=pl.ANY)] * 2,
         out_specs=pl.BlockSpec(memory_space=pltpu.VMEM),
         scratch_shapes=[
+            pltpu.VMEM((tok, width), jnp.bfloat16),
+            pltpu.VMEM((1, tok), jnp.int32),
             pltpu.VMEM((4, tok, width), jnp.bfloat16),
-            pltpu.VMEM((4, tok, width), jnp.bfloat16),
+            pltpu.VMEM((4 * tok, width), jnp.bfloat16),
             pltpu.VMEM((RELAYED, tok // CHUNKS, width), jnp.bfloat16),
+            pltpu.VMEM((1, tok), jnp.float32),
             pltpu.VMEM((16, 1, tok), jnp.int32),
-            pltpu.VMEM((4, tok, LANES), jnp.int32),
-            pltpu.VMEM((4, tok, LANES), jnp.float32),
+            pltpu.VMEM((4 * tok, LANES), jnp.int32),
+            pltpu.VMEM((4 * tok, LANES), jnp.float32),
             pltpu.VMEM((4, 1, tok), jnp.float32),
             pltpu.VMEM((4, 1, tok), jnp.float32),
             pltpu.VMEM((16, 1, tok), jnp.float32),
@@ -474,9 +505,10 @@
             pltpu.SemaphoreType.DMA((RELAYED,)),
             pltpu.SemaphoreType.DMA((RELAYED,)),
             pltpu.SemaphoreType.DMA((10,)),
+            pltpu.SemaphoreType.DMA((2,)),
         ],
         compiler_params=pltpu.CompilerParams(
-            collective_id=0, has_side_effects=True, vmem_limit_bytes=40 << 20),
+            collective_id=0, has_side_effects=True, vmem_limit_bytes=60 << 20),
     )(embeddings, assignment.reshape(1, tok))
     return score.reshape(tok)
 

time: 60.2 us -> 55.3 us (0.919)
  Pallas kernels: 57.5 us -> 53.9 us
  local copies, waits for them, and re-layouts: 2.49 us -> 1.26 us
    pallas_call x1, Pallas kernels: 57.5 us -> 53.9 us  [pair_scores(): pl.pallas_call(pair_kernel, out_shape=jax.ShapeDtypeStruct((1, tok), jnp....]
    unnamed x5 -> x1, local copies, waits for them, and re-layouts: 2.49 us -> 1.26 us
where the time goes in v3:
time: 55.3 us; the launch traced here: 55.1 us
  Pallas kernels  53.9 us (97%)
  local copies, waits for them, and re-layouts  1.26 us (2%)
    pallas_call x1, Pallas kernels, pair_scores(): pl.pallas_call(pair_kernel, out_shape=jax.ShapeDtypeStruct((1, tok), jnp....  53.9 us
    unnamed x1, local copies, waits for them, and re-layouts  1.26 us

profile of v3, /device:TPU:0, one launch (start us, length us, event | category | flops | bytes accessed | tf_op | source)
XLA Modules:
  0.0 55.1 jit_solution(12356169034923346824)
XLA Ops:
  0.0 53.9 %shard_map.28 = f32[1,512]{1,0:T(1,128)} custom-call(bf16[512,1024]{1,0:T(8,128)(2,1)} %emb_hbm.1, s32[1,512]{1,0:T(1,128)} %bitcast.3), custom_call_target="tpu_custom_call" | custom-call | tf_op jit(solution)/shard_map/pallas_call | solution.py:479
  53.9 1.3 %copy.4 = f32[512]{0:T(512)} copy(f32[512]{0:T(512)} %bitcast.2) | data formatting | bytes 4096
